TPU v7x, 128 devices: a whole 4x4x4 slice. The times are simulated.
128 devices in a mesh: grp: 4 (over y_lo, core), dev: 32 (over z, y_hi, x).
Axes of the slice: x: 4, y: 4 (y_hi: 2, y_lo: 2; y = y_hi * 2 + y_lo), z: 4, core: 2. Of those that a mesh axis runs over, the one named last changes fastest.
Arguments:
- tokens: bfloat16 [1536, 4096], P(None, 'dev'), may hold values from -30 to 30
- in_weight: bfloat16 [4096, 16384], P(None, 'dev'), may hold values from -0.09375 to 0.09375
- upstream: bfloat16 [1536, 16384], P(None, 'dev'), may hold values from -30 to 30
- slot_block: int32 [256], P('dev'), may hold values from 0 to 255, as said below
- refreshed: int32 [32], replicated, may hold values from 0 to 255, as said below
- statistics: bfloat16 [256, 2, 512, 512], P('dev'), may hold values from -60 to 90, as said below
- roots: bfloat16 [256, 2, 512, 512], P('dev'), may hold values from 0 to 8, as said below
Outputs:
- update: bfloat16 [256, 512, 512], P('dev', 'grp')
Inputs may be any that keep to these rules, and one draw needn't show every extreme that they name: `slot_block`: a permutation of the 256 block ids; slot s belongs to owner s // 8. `refreshed`: 32 distinct block ids; at most 2 of them are held in the slots of one owner, and some owner holds exactly 2. `statistics`: each [512, 512] matrix is symmetric. `roots`: each [512, 512] matrix is symmetric.
All inputs are finite; a program needn't handle non-finite values.
Results may differ from a plain program's by a relative error of at most 0.02.
Values may be sent and summed in bfloat16 or wider, within the bound.
No kernel may reach another device: no remote copies, remote signals or barrier semaphores. Data moves between devices by JAX's collectives and lax.ppermute only.
A program may use at most 128 MiB of HBM per device.

v0:
```python
import jax
import jax.numpy as jnp
from jax import lax
from jax.sharding import PartitionSpec as P

ITERS = 3
MOSTR = 2


decay = 0.9
jitter = 1e-06
floor_eps = 1e-06


def spread(block, axis, holder):
    block = jnp.where(lax.axis_index(axis) == holder, block, jnp.zeros_like(block))
    return lax.psum(block, axis)


def gelu_slope(values):
    return (
        0.5 * (1.0 + lax.erf(values * 0.7071067811865476))
        + values * jnp.exp(-0.5 * values * values) * 0.3989422804014327
    )


def inverse_root(matrices):
    order = matrices.shape[-1]
    identity = jnp.eye(order, dtype=matrices.dtype)
    trace_value = jnp.trace(matrices, axis1=-2, axis2=-1)[..., None, None]
    power = matrices / trace_value
    result = None
    for sweep in range(ITERS):
        factor = (5.0 * identity - power) * 0.25
        if result is None:
            result = factor
        else:
            result = jnp.matmul(result, factor, precision=lax.Precision.HIGHEST)
        if sweep + 1 < ITERS:
            square = jnp.matmul(factor, factor, precision=lax.Precision.HIGHEST)
            fourth = jnp.matmul(square, square, precision=lax.Precision.HIGHEST)
            power = jnp.matmul(fourth, power, precision=lax.Precision.HIGHEST)
    return result


def kronecker_pair(stats_pair, grads):
    order = grads.shape[-1]
    identity = jnp.eye(order, dtype=jnp.float32)
    left_outer = jnp.einsum("kij,klj->kil", grads, grads, preferred_element_type=jnp.float32)
    right_outer = jnp.einsum("kji,kjl->kil", grads, grads, preferred_element_type=jnp.float32)
    outer = jnp.stack([left_outer, right_outer], axis=1)
    return decay * stats_pair.astype(jnp.float32) + outer + jitter * identity


def precondition(factors, grads):
    first = jnp.einsum(
        "kab,kbc->kac", factors[:, 0], grads, preferred_element_type=jnp.float32
    ).astype(jnp.bfloat16)
    second = jnp.einsum("kab,kbc->kac", first, factors[:, 1], preferred_element_type=jnp.float32)
    mean_square = jnp.mean(second * second, axis=(1, 2), keepdims=True)
    return (second * lax.rsqrt(mean_square + floor_eps)).astype(jnp.bfloat16)


def shards(tokens, in_weight, upstream, slot_block, refreshed, statistics, roots):
    group = lax.axis_index("grp")
    ngroups = lax.axis_size("grp")
    last_group = ngroups - 1
    trainers = ngroups - 1
    columns = lax.axis_size("dev")
    total_tokens = tokens.shape[0]
    group_tokens = total_tokens // trainers
    width = in_weight.shape[1]
    slot_count = statistics.shape[0]
    start_row = jnp.minimum(group, trainers - 1) * group_tokens
    own_tokens = lax.dynamic_slice_in_dim(tokens, start_row, group_tokens, 0)
    own_upstream = lax.dynamic_slice_in_dim(upstream, start_row, group_tokens, 0)
    piece = lax.all_gather(own_tokens, "dev", axis=1, tiled=True)
    forward_sum = jnp.dot(piece, in_weight, preferred_element_type=jnp.float32)
    delta = (own_upstream.astype(jnp.float32) * gelu_slope(forward_sum)).astype(jnp.bfloat16)
    all_delta = lax.all_gather(delta, "dev", axis=1, tiled=True)
    block_rows = slot_block // columns
    block_cols = slot_block % columns
    left_cut = jax.vmap(
        lambda block_row: lax.dynamic_slice_in_dim(piece, block_row * width, width, 1)
    )(block_rows)
    right_cut = jax.vmap(
        lambda block_col: lax.dynamic_slice_in_dim(all_delta, block_col * width, width, 1)
    )(block_cols)
    partial_value = (
        jnp.einsum("ktr,ktc->krc", left_cut, right_cut, preferred_element_type=jnp.float32)
        / total_tokens
    ).astype(jnp.bfloat16)
    partial_value = jnp.where(group < trainers, partial_value, jnp.zeros_like(partial_value))
    grads = lax.psum(partial_value, "grp").astype(jnp.float32).astype(jnp.bfloat16)
    matches = slot_block[:, None] == refreshed[None, :]
    is_fresh = jnp.any(matches, axis=1)
    fresh_flags = is_fresh.astype(jnp.int32)
    ranks = jnp.cumsum(fresh_flags) - fresh_flags
    positions = jnp.arange(MOSTR, dtype=jnp.int32)
    selector = is_fresh[None, :] & (ranks[None, :] == positions[:, None])
    picks = jnp.sum(
        selector.astype(jnp.int32) * jnp.arange(slot_count, dtype=jnp.int32)[None, :], axis=1
    )
    rank_clip = jnp.minimum(ranks, MOSTR - 1)

    def refresh(slot_picks):
        grads_pick = jnp.take(grads, slot_picks, axis=0)
        stats_pick = jnp.take(statistics, slot_picks, axis=0)
        return inverse_root(kronecker_pair(stats_pick, grads_pick)).astype(jnp.bfloat16)

    def assemble(fresh_roots):
        chosen = jnp.take(fresh_roots, rank_clip, axis=0)
        merged = jnp.where(is_fresh[:, None, None, None], chosen, roots)
        return precondition(merged, grads)

    def owner_work(unused):
        return assemble(refresh(picks))

    def spare_work(unused):
        return jnp.zeros(grads.shape, jnp.bfloat16)

    local_update = lax.cond(group == last_group, owner_work, spare_work, 0)
    update = spread(local_update, "grp", last_group)
    slice_rows = width // ngroups
    return lax.dynamic_slice_in_dim(update, group * slice_rows, slice_rows, 1)


def solution(mesh):
    return jax.shard_map(
        shards,
        mesh=mesh,
        in_specs=(
            P(None, "dev"),
            P(None, "dev"),
            P(None, "dev"),
            P("dev"),
            P(),
            P("dev", None, None, None),
            P("dev", None, None, None),
        ),
        out_specs=P("dev", "grp", None),
        check_vma=False,
    )
```

profile of v0, /device:TPU:1, one launch (start us, length us, event | category | flops | bytes accessed | tf_op | source)
XLA Modules:
  0.0 595.7 jit_solution(18259073017818057094)
XLA Ops:
  6.5 1.0 copy-done
  7.5 0.7 constant_dynamic-slice_fusion.3
  8.3 85.9 %all-gather.3.cloned.1.call-done = bf16[512,4096]{1,0:T(8,128)(2,1)} async-done(((bf16[512,128]{1,0:T(8,128)(2,1)}), bf16[512,4096]{1,0:T(8,128)(2,1)}) %all-gather.3.cloned.1.call-update) | async-done | bytes 4194320 | tf_op jit(solution)/shard_map/all_gather | solution.py:77
  94.2 6.9 %fusion.34 = bf16[512,512]{1,0:T(8,128)(2,1)} fusion(bf16[1536,512]{1,0:T(8,128)(2,1)} %param.11, s32[]{:T(128)S(6)} %select_n.80, bf16[512,4096]{1,0:T(8,128)(2,1)} %all-gather.3.cloned.1.call-done, bf16[4096,512]{1,0:T(8,128)(2,1)} %param.10), kind=kOutput, calls=%fused_computation.68 | convolution fusion | flops 2150367232 | bytes 9437188 | tf_op jit(solution)/shard_map/dot_general | solution.py:78
  101.2 2.3 broadcast.145.clone
  103.6 28.1 %while.2 = (s32[]{:T(128)}, bf16[512,4096]{1,0:T(8,128)(2,1)}, s32[8,2]{0,1:T(2,128)S(1)}, bf16[8,512,512]{2,1,0:T(8,128)(2,1)}, s32[]{:T(128)}) while((s32[]{:T(128)}, bf16[512,4096]{1,0:T(8,128)(2,1)}, s32[8,2]{0,1:T(2,128)S(1)}, bf16[8,512,512]{2,1,0:T(8,128)(2,1)}, s32[]{:T(128)}) %tuple.41), condition=%wide.while_cond, body=%wide.while_body.sunk | while | flops 2 | bytes 1049689 | solution.py:84
  103.7 0.6 slice.50
  104.2 2.8 bitcast_dynamic-update-slice_fusion.4
  107.2 0.6 slice.50
  107.7 2.8 bitcast_dynamic-update-slice_fusion.4
  110.7 0.6 slice.50
  111.2 2.9 bitcast_dynamic-update-slice_fusion.4
  114.2 0.6 slice.50
  114.8 2.8 bitcast_dynamic-update-slice_fusion.4
  117.7 0.6 slice.50
  118.3 2.9 bitcast_dynamic-update-slice_fusion.4
  121.2 0.6 slice.50
  121.8 2.9 bitcast_dynamic-update-slice_fusion.4
  124.7 0.6 slice.50
  125.3 2.8 bitcast_dynamic-update-slice_fusion.4
  128.2 0.6 slice.50
  128.8 2.9 bitcast_dynamic-update-slice_fusion.4
  131.7 118.1 %all-gather.5.cloned.1.call-done = bf16[512,16384]{1,0:T(8,128)(2,1)} async-done(((bf16[512,512]{1,0:T(8,128)(2,1)}), bf16[512,16384]{1,0:T(8,128)(2,1)}) %all-gather.5.cloned.1.call-update) | async-done | bytes 16777232 | tf_op jit(solution)/shard_map/all_gather | solution.py:80
  249.8 2.3 broadcast.145.clone.1
  252.1 27.2 %while.3 = (s32[]{:T(128)}, bf16[512,16384]{1,0:T(8,128)(2,1)}, s32[8,2]{0,1:T(2,128)S(1)}, bf16[8,512,512]{2,1,0:T(8,128)(2,1)}, s32[]{:T(128)}) while((s32[]{:T(128)}, bf16[512,16384]{1,0:T(8,128)(2,1)}, s32[8,2]{0,1:T(2,128)S(1)}, bf16[8,512,512]{2,1,0:T(8,128)(2,1)}, s32[]{:T(128)}) %tuple.44), condition=%wide.while_cond.1, body=%wide.while_body.1.sunk | while | flops 2 | bytes 1049689 | solution.py:87
  252.2 0.5 slice.51
  252.7 2.8 bitcast_dynamic-update-slice_fusion.5
  255.6 0.5 slice.51
  256.1 2.8 bitcast_dynamic-update-slice_fusion.5
  259.0 0.5 slice.51
  259.5 2.8 bitcast_dynamic-update-slice_fusion.5
  262.4 0.5 slice.51
  262.9 2.8 bitcast_dynamic-update-slice_fusion.5
  265.8 0.5 slice.51
  266.3 2.8 bitcast_dynamic-update-slice_fusion.5
  269.2 0.5 slice.51
  269.7 2.8 bitcast_dynamic-update-slice_fusion.5
  272.6 0.5 slice.51
  273.1 2.8 bitcast_dynamic-update-slice_fusion.5
  276.5 2.8 bitcast_dynamic-update-slice_fusion.5
  279.3 7.8 %fusion.28 = bf16[8,512,512]{2,1,0:T(8,128)(2,1)} fusion(pred[]{:T(512)S(6)} %lt.39, bf16[8,512,512]{2,1,0:T(8,128)(2,1)} %get-tuple-element.66, bf16[8,512,512]{2,1,0:T(8,128)(2,1)} %get-tuple-element.74), kind=kOutput, calls=%fused_computation.60 | convolution fusion | flops 2153775104 | bytes 12582913 | tf_op jit(solution)/shard_map/ktr,ktc->krc/dot_general | solution.py:90
  287.2 0.6 copy-done.5
  288.1 89.2 %all-reduce.5.cloned.1.call-done = bf16[8,512,512]{2,1,0:T(8,128)(2,1)} async-done(((bf16[8,512,512]{2,1,0:T(8,128)(2,1)}), bf16[8,512,512]{2,1,0:T(8,128)(2,1)}) %all-reduce.5.cloned.1.call-update) | async-done | bytes 4194320 | tf_op jit(solution)/shard_map/psum | solution.py:94
  377.4 2.3 conditional.1
  377.4 2.3 broadcast.120
  379.7 2.2 broadcast_select_fusion.3
  381.9 205.0 %all-reduce.7.cloned.1.call-done = bf16[8,512,512]{2,1,0:T(8,128)(2,1)} async-done(((bf16[8,512,512]{2,1,0:T(8,128)(2,1)}), bf16[8,512,512]{2,1,0:T(8,128)(2,1)}) %all-reduce.7.cloned.1.call-update) | async-done | bytes 4194320 | tf_op jit(solution)/shard_map/psum | solution.py:17
  586.9 2.3 constant_dynamic-slice_fusion.2
  (40 shorter events, 2.3 us)
Async XLA Ops:
  6.5 1.0 copy-start
  6.5 87.6 %all-gather.3.cloned.1.call-start = ((), (), s32[]{:S(2)}) async-start(), calls=%async_computation | async-start | bytes 4325376 | tf_op jit(solution)/shard_map/all_gather | solution.py:77
  8.2 92.9 %copy-start.4 = (s32[8]{0:T(128)S(1)}, s32[8]{0:T(128)}, u32[]{:S(2)}) copy-start(s32[8]{0:T(128)} %param.12) | copy-start | bytes 100
  8.2 241.6 %all-gather.5.cloned.1.call-start = ((), (), s32[]{:S(2)}) async-start(), calls=%async_computation.1 | async-start | bytes 17301504 | tf_op jit(solution)/shard_map/all_gather | solution.py:80
  101.1 276.2 %all-reduce.5.cloned.1.call-start = ((), (), s32[]{:S(2)}) async-start(), calls=%async_computation.2 | async-start | bytes 8388608 | tf_op jit(solution)/shard_map/psum | solution.py:94
  287.1 0.7 copy-start.5
  287.1 299.8 %all-reduce.7.cloned.1.call-start = ((), (), s32[]{:S(2)}) async-start(), calls=%async_computation.3 | async-start | bytes 8388608 | tf_op jit(solution)/shard_map/psum | solution.py:17
  379.7 209.5 %copy-start.1 = (bf16[1536,128]{1,0:T(8,128)(2,1)S(1)}, bf16[1536,128]{1,0:T(8,128)(2,1)}, u32[]{:S(2)}) copy-start(bf16[1536,128]{1,0:T(8,128)(2,1)} %param.9) | copy-start | bytes 1179652
Sparse Core Ops, SparseCore 0:
  10.1 83.9 all-gather.2
  101.2 148.5 all-gather.4
  287.3 90.0 all-reduce.4
  382.1 204.8 all-reduce.6
where the time goes:
time: 604 us; the launch traced here: 596 us
  waiting for transfers between devices  498 us (82%)
  local copies, waits for them, and re-layouts  66.8 us (11%)
  matrix products  14.8 us (2%)
  between operations  13.2 us (2%)
    psum x1, waiting for transfers between devices, spread(): return lax.psum(block, axis)  205 us
    all_gather x1, waiting for transfers between devices, shards(): all_delta = lax.all_gather(delta, 'dev', axis=1, tiled=True)  118 us
    psum x1, waiting for transfers between devices, shards(): lax.psum(partial_value, 'grp').astype(jnp.float32).astype(jnp.bfloat16)  89.2 us
    all_gather x1, waiting for transfers between devices, shards(): piece = lax.all_gather(own_tokens, 'dev', axis=1, tiled=True)  85.9 us
    gather x48, local copies, waits for them, and re-layouts  55.3 us
  transfers between devices with their start and end apart: 4, of which 4 were waited for; matrix products, arithmetic and copies ran while one was open for 5% of the time, Pallas kernels for 0%

commit v1 on v0

v1 whole, which is shorter than its diff:
```python
import jax
import jax.numpy as jnp
from jax import lax
from jax.experimental import pallas as pl
from jax.experimental.pallas import tpu as pltpu
from jax.sharding import PartitionSpec as P

decay = 0.9
jitter = 1e-06
floor_eps = 1e-06

ROWS = 384
IDS = 16
BLOCK = 512
BF = jnp.bfloat16
F32 = jnp.float32
MIB = 1 << 20

CORE = [(0, 1), (1, 0), (2, 3), (3, 2)]
CHIP = [(0, 2), (2, 0), (1, 3), (3, 1)]
SAME_CORE = [[chip * 64 + core * 32 + d for chip in range(2) for d in range(32)] for core in range(2)]


def params(mib):
    return pltpu.CompilerParams(vmem_limit_bytes=mib * MIB)


def nt(a, b):
    return lax.dot_general(a, b, (((1,), (1,)), ((), ())), preferred_element_type=F32)


def nn(a, b):
    return jnp.dot(a, b, preferred_element_type=F32)


def unit(n, dtype):
    row = lax.broadcasted_iota(jnp.int32, (n, n), 0)
    col = lax.broadcasted_iota(jnp.int32, (n, n), 1)
    return jnp.where(row == col, 1.0, 0.0).astype(dtype)


def gelu_slope(values):
    return (
        0.5 * (1.0 + lax.erf(values * 0.7071067811865476))
        + values * jnp.exp(-0.5 * values * values) * 0.3989422804014327
    )


def spare_position(k):
    return jnp.where(k < 3, 7 - k, jnp.where(k < 6, 6 - k, jnp.where(k == 6, 4, 0)))


def place(is_fresh, fresh_seen, spare_seen):
    position = jnp.where(is_fresh, 4 * fresh_seen, spare_position(spare_seen))
    return jnp.minimum(position, 7)


def mark_fresh(refreshed, table):
    def clear(k, c):
        table[k] = 0
        return c

    def mark(k, c):
        table[refreshed[k]] = 1
        return c

    lax.fori_loop(0, 256, clear, 0, unroll=8)
    lax.fori_loop(0, 32, mark, 0, unroll=8)


def plan_kernel(slot_block, refreshed, slot_at, table):
    mark_fresh(refreshed, table)
    fresh_seen = jnp.int32(0)
    spare_seen = jnp.int32(0)
    for p in range(8):
        flag = table[slot_block[p]]
        slot_at[place(flag == 1, fresh_seen, spare_seen)] = p
        fresh_seen += flag
        spare_seen += 1 - flag
    slot_at[8] = fresh_seen


def plan(slot_block, refreshed):
    smem = pl.BlockSpec(memory_space=pltpu.SMEM)
    return pl.pallas_call(
        plan_kernel,
        out_shape=jax.ShapeDtypeStruct((16,), jnp.int32),
        in_specs=[smem, smem],
        out_specs=smem,
        scratch_shapes=[pltpu.SMEM((256,), jnp.int32)],
        name="plan",
    )(slot_block, refreshed)


def wide(ref):
    return jnp.concatenate([ref[j][:ROWS] for j in range(ref.shape[0])], axis=1)


def gradient_kernel(where, own, other, weight, up_own, up_other, out, acc, delta_t):
    step = pl.program_id(0)

    @pl.when(step == 0)
    def _():
        acc[...] = jnp.zeros_like(acc)

    @pl.when(step < 4)
    def _():
        acc[:ROWS] += nn(wide(own), weight[...])
        acc[ROWS:] += nn(wide(other), weight[...])

    @pl.when(step == 3)
    def _():
        eye = unit(256, BF)
        for half, up in ((0, up_own), (1, up_other)):
            rows = pl.ds(half * ROWS, ROWS)
            delta = (up[...].astype(F32) * gelu_slope(acc[rows])).astype(BF)
            delta_t[:, rows] = nt(eye, delta).astype(BF)

    @pl.when(step >= 4)
    def _():
        both = jnp.concatenate([wide(own), wide(other)], axis=0)
        part = (nn(delta_t[...], both) / 1536.0).astype(BF)
        for row in range(2):
            for quarter in range(4):
                start = row * BLOCK + quarter * 128
                out[quarter * 16 : (quarter + 1) * 16, row] = part[:, start : start + 128].reshape(16, 16, 128)


def gradient_pieces(where, own, other, in_weight, upstream):
    rows = ROWS + IDS
    return pl.pallas_call(
        gradient_kernel,
        out_shape=jax.ShapeDtypeStruct((64, 8, 16, 128), BF),
        grid_spec=pltpu.PrefetchScalarGridSpec(
            num_scalar_prefetch=1,
            grid=(8,),
            in_specs=[
                pl.BlockSpec((8, rows, 128), lambda i, w: (i % 4, 0, 0)),
                pl.BlockSpec((8, rows, 128), lambda i, w: (i % 4, 0, 0)),
                pl.BlockSpec((1024, 256), lambda i, w: (jnp.minimum(i, 3), w[1])),
                pl.BlockSpec((ROWS, 256), lambda i, w: (w[0], w[1])),
                pl.BlockSpec((ROWS, 256), lambda i, w: (w[2], w[1])),
            ],
            out_specs=pl.BlockSpec((64, 2, 16, 128), lambda i, w: (0, jnp.maximum(i - 4, 0), 0, 0)),
            scratch_shapes=[pltpu.VMEM((2 * ROWS, 256), F32), pltpu.VMEM((256, 2 * ROWS), BF)],
        ),
        compiler_params=params(40),
        name="gradient",
    )(where, own, other, in_weight, upstream, upstream)


def route_kernel(ids, refreshed, pieces, out, table):
    mark_fresh(refreshed, table)

    def owner(o, c):
        fresh_seen = jnp.int32(0)
        spare_seen = jnp.int32(0)
        for p in range(8):
            block = ids[o * 8 + p]
            flag = table[block]
            position = place(flag == 1, fresh_seen, spare_seen)
            fresh_seen += flag
            spare_seen += 1 - flag
            row, col = block // 32, block % 32
            total = pieces[col, row].astype(F32) + pieces[col + 32, row].astype(F32)
            out[(position // 4) * 32 + o, position % 4] = total.astype(BF)
        return c

    lax.fori_loop(0, 32, owner, 0)


def route(ids, refreshed, pieces):
    smem = pl.BlockSpec(memory_space=pltpu.SMEM)
    vmem = pl.BlockSpec(memory_space=pltpu.VMEM)
    return pl.pallas_call(
        route_kernel,
        out_shape=jax.ShapeDtypeStruct((64, 4, 16, 128), BF),
        in_specs=[smem, smem, vmem],
        out_specs=vmem,
        scratch_shapes=[pltpu.SMEM((256,), jnp.int32)],
        compiler_params=params(16),
        name="route",
    )(ids, refreshed, pieces)


def collect(core, mine, theirs, grad_t):
    for quarter in range(4):
        cols = slice(quarter * 128, (quarter + 1) * 128)
        part = slice(quarter * 16, (quarter + 1) * 16)
        grad_t[pl.ds(pl.multiple_of(core * 256, 256), 256), cols] = mine[part, 0].reshape(256, 128)
        grad_t[pl.ds(pl.multiple_of(256 - core * 256, 256), 256), cols] = theirs[part, 0].reshape(256, 128)


def precondition(left, right, grad_t):
    first = nt(left, grad_t).astype(BF)
    second = nn(first, right)
    mean_square = jnp.sum(second * second, keepdims=True) * (1.0 / (BLOCK * BLOCK))
    return second * lax.rsqrt(mean_square + floor_eps)


def hand_out(where, value, keep, send, full):
    full[...] = value
    keep[0] = full[pl.ds(pl.multiple_of(where[0] * 128, 128), 128)].astype(BF)
    send[0] = full[pl.ds(pl.multiple_of(where[3] * 128, 128), 128)].astype(BF)


def stored_kernel(where, slot_at, mine, theirs, roots, keep, send, grad_t, full):
    collect(where[1], mine, theirs, grad_t)
    hand_out(where, precondition(roots[0, 0], roots[0, 1], grad_t[...]), keep, send, full)


def stored_slots(where, slot_at, mine, theirs, roots):
    half = pl.BlockSpec((64, 1, 16, 128), lambda i, w, s: (0, i + 1, 0, 0))
    rows = pl.BlockSpec((1, 128, BLOCK), lambda i, w, s: (i, 0, 0))
    return pl.pallas_call(
        stored_kernel,
        out_shape=[jax.ShapeDtypeStruct((3, 128, BLOCK), BF)] * 2,
        grid_spec=pltpu.PrefetchScalarGridSpec(
            num_scalar_prefetch=2,
            grid=(3,),
            in_specs=[half, half, pl.BlockSpec((1, 2, BLOCK, BLOCK), lambda i, w, s: (s[w[4] + i + 1], 0, 0, 0))],
            out_specs=[rows, rows],
            scratch_shapes=[pltpu.VMEM((BLOCK, BLOCK), BF), pltpu.VMEM((BLOCK, BLOCK), F32)],
        ),
        compiler_params=params(32),
        name="stored",
    )(where, slot_at, mine, theirs, roots)


def split(a):
    high = a.astype(BF)
    return high, (a - high.astype(F32)).astype(BF)


def product(a, b):
    ah, al = a
    bh, bl = b
    return nn(ah, bh) + (nn(ah, bl) + nn(al, bh))


def inverse_root(matrix):
    eye = unit(BLOCK, F32)
    power = matrix / jnp.sum(matrix * eye, keepdims=True)
    factor0 = (5.0 * eye - power) * 0.25
    f0 = split(factor0)
    s = split(product(f0, f0))
    q = split(product(s, s))
    power = product(q, split(power))
    factor1 = (5.0 * eye - power) * 0.25
    f1 = split(factor1)
    result = split(product(f0, f1))
    s = split(product(f1, f1))
    q = split(product(s, s))
    power = product(q, split(power))
    factor2 = (5.0 * eye - power) * 0.25
    return product(result, split(factor2))


def newton_kernel(where, slot_at, mine, theirs, statistic, out, grad_t):
    core = where[1]
    collect(core, mine, theirs, grad_t)

    @pl.when(core == 0)
    def _():
        grad_t[...] = nt(unit(BLOCK, BF), grad_t[...]).astype(BF)

    g = grad_t[...]
    matrix = decay * statistic[0, 0].astype(F32) + nt(g, g) + jitter * unit(BLOCK, F32)
    out[...] = inverse_root(matrix).astype(BF)


def newton(where, slot_at, mine, theirs, statistics):
    half = pl.BlockSpec((64, 1, 16, 128), lambda i, w, s: (0, 0, 0, 0))
    return pl.pallas_call(
        newton_kernel,
        out_shape=jax.ShapeDtypeStruct((BLOCK, BLOCK), BF),
        grid_spec=pltpu.PrefetchScalarGridSpec(
            num_scalar_prefetch=2,
            grid=(1,),
            in_specs=[half, half, pl.BlockSpec((1, 1, BLOCK, BLOCK), lambda i, w, s: (s[w[4]], w[1], 0, 0))],
            out_specs=pl.BlockSpec((BLOCK, BLOCK), lambda i, w, s: (0, 0)),
            scratch_shapes=[pltpu.VMEM((BLOCK, BLOCK), BF)],
        ),
        compiler_params=params(48),
        name="newton",
    )(where, slot_at, mine, theirs, statistics)


def fresh_kernel(where, slot_at, mine, theirs, roots, root, other_root, keep, send, grad_t, full, pair):
    core = where[1]
    collect(core, mine, theirs, grad_t)
    pair[...] = roots[0]

    @pl.when(slot_at[8] > where[4] // 4)
    def _():
        pair[core] = root[...]
        pair[1 - core] = other_root[...]

    hand_out(where, precondition(pair[0], pair[1], grad_t[...]), keep, send, full)


def fresh_slot(where, slot_at, mine, theirs, roots, root, other_root):
    half = pl.BlockSpec((64, 1, 16, 128), lambda i, w, s: (0, 0, 0, 0))
    rows = pl.BlockSpec((1, 128, BLOCK), lambda i, w, s: (0, 0, 0))
    square = pl.BlockSpec((BLOCK, BLOCK), lambda i, w, s: (0, 0))
    return pl.pallas_call(
        fresh_kernel,
        out_shape=[jax.ShapeDtypeStruct((1, 128, BLOCK), BF)] * 2,
        grid_spec=pltpu.PrefetchScalarGridSpec(
            num_scalar_prefetch=2,
            grid=(1,),
            in_specs=[
                half,
                half,
                pl.BlockSpec((1, 2, BLOCK, BLOCK), lambda i, w, s: (s[w[4]], 0, 0, 0)),
                square,
                square,
            ],
            out_specs=[rows, rows],
            scratch_shapes=[
                pltpu.VMEM((BLOCK, BLOCK), BF),
                pltpu.VMEM((BLOCK, BLOCK), F32),
                pltpu.VMEM((2, BLOCK, BLOCK), BF),
            ],
        ),
        compiler_params=params(32),
        name="fresh",
    )(where, slot_at, mine, theirs, roots, root, other_root)


def assemble_kernel(where, slot_at, fresh_mine, fresh_theirs, mine, theirs, out):
    here = where[4]
    there = 4 - here
    out[slot_at[here]] = fresh_mine[0]
    out[slot_at[there]] = fresh_theirs[0]
    for k in range(3):
        out[slot_at[here + k + 1]] = mine[k]
        out[slot_at[there + k + 1]] = theirs[k]


def assemble(where, slot_at, *parts):
    smem = pl.BlockSpec(memory_space=pltpu.SMEM)
    vmem = pl.BlockSpec(memory_space=pltpu.VMEM)
    return pl.pallas_call(
        assemble_kernel,
        out_shape=jax.ShapeDtypeStruct((8, 128, BLOCK), BF),
        in_specs=[smem, smem] + [vmem] * 4,
        out_specs=vmem,
        compiler_params=params(16),
        name="assemble",
    )(where, slot_at, *parts)


def shards(tokens, in_weight, upstream, slot_block, refreshed, statistics, roots):
    group = lax.axis_index("grp")
    core = group % 2
    chip = group // 2
    both = ("grp", "dev")
    where = jnp.stack([group, core, group + 1 - 2 * core, group + 2 - 4 * chip, 4 * chip]).astype(jnp.int32)
    slot_at = plan(slot_block, refreshed)

    own = lax.dynamic_slice_in_dim(tokens, group * ROWS, ROWS, 0)
    ids = jnp.pad(slot_block.astype(BF).reshape(1, 8), ((0, IDS - 1), (0, 120)))
    sent = jnp.broadcast_to(jnp.concatenate([own, ids], axis=0)[None], (32, ROWS + IDS, 128))
    features = lax.all_to_all(sent, "dev", 0, 0, tiled=True)
    all_ids = features[:, ROWS, :8].astype(jnp.int32).reshape(256)
    other_features = lax.ppermute(features, "grp", CORE)

    pieces = gradient_pieces(where, features, other_features, in_weight, upstream)
    pieces = lax.all_to_all(pieces, both, 0, 0, tiled=True, axis_index_groups=SAME_CORE)
    pieces = route(all_ids, refreshed, pieces)
    mine = lax.all_to_all(pieces, both, 0, 0, tiled=True, axis_index_groups=SAME_CORE)
    theirs = lax.ppermute(mine, "grp", CORE)

    keep, send = stored_slots(where, slot_at, mine, theirs, roots)
    other_keep = lax.ppermute(send, "grp", CHIP)
    root = newton(where, slot_at, mine, theirs, statistics)
    other_root = lax.ppermute(root, "grp", CORE)
    fresh_keep, fresh_send = fresh_slot(where, slot_at, mine, theirs, roots, root, other_root)
    fresh_other = lax.ppermute(fresh_send, "grp", CHIP)
    return assemble(where, slot_at, fresh_keep, fresh_other, keep, other_keep)


def solution(mesh):
    return jax.shard_map(
        shards,
        mesh=mesh,
        in_specs=(
            P(None, "dev"),
            P(None, "dev"),
            P(None, "dev"),
            P("dev"),
            P(),
            P("dev", None, None, None),
            P("dev", None, None, None),
        ),
        out_specs=P("dev", "grp", None),
        check_vma=False,
    )
```

time: 604 us -> 178 us (0.29); the launches traced: 596 us -> 177 us
  waiting for transfers between devices: 498 us -> 40.4 us
  blocking collectives: 0 us -> 75.4 us
  local copies, waits for them, and re-layouts: 66.8 us -> 10.5 us
  Pallas kernels: 0 us -> 36 us
  matrix products: 14.8 us -> 0 us
  between operations: 13.2 us -> 0.09 us
  starting transfers between devices: 0.13 us -> 13 us
    psum x2 -> x0, waiting for transfers between devices: 294 us -> none  [the longest x1 205 us: spread(): return lax.psum(block, axis)]
    all_gather x2 -> x0, waiting for transfers between devices: 204 us -> none  [the longest x1 118 us: shards(): all_delta = lax.all_gather(delta, 'dev', axis=1, tiled=True)]
    all_to_all x0 -> x2, blocking collectives: none -> 75.4 us  [the longest x1 53.4 us: shards(): features = lax.all_to_all(sent, 'dev', 0, 0, tiled=True)]
    gather x48 -> x0, local copies, waits for them, and re-layouts: 55.3 us -> none
    pallas_call x0 -> x7, Pallas kernels: none -> 36 us  [the longest x1 11.1 us: gradient_pieces(): pl.pallas_call(gradient_kernel, out_shape=jax.ShapeDtypeStruct((64, 8, 16...]
    all_to_all x0 -> x1, waiting for transfers between devices: none -> 27.3 us  [shards(): lax.all_to_all(pieces, both, 0, 0, tiled=True, axis_index_groups=SAME_CORE)]
    dot_general x2 -> x0, matrix products: 14.8 us -> none  [the longest x1 7.84 us: shards(): jnp.einsum('ktr,ktc->krc', left_cut, right_cut, preferred_element_type=jn...]
    ppermute x0 -> x5, waiting for transfers between devices: none -> 13.1 us  [the longest x1 5.73 us: shards(): other_features = lax.ppermute(features, 'grp', CORE)]
  transfers between devices with their start and end apart: 4 -> 6, of which waited for: 4 -> 5; matrix products, arithmetic and copies ran while one was open for 5% -> 1% of each run, Pallas kernels for 0% -> 4%
where the time goes in v1:
time: 178 us; the launch traced here: 177 us
  blocking collectives  75.4 us (42%)
  waiting for transfers between devices  40.4 us (23%)
  Pallas kernels  36 us (20%)
  starting transfers between devices  13 us (7%)
  local copies, waits for them, and re-layouts  10.5 us (6%)
    all_to_all x1, blocking collectives, shards(): features = lax.all_to_all(sent, 'dev', 0, 0, tiled=True)  53.4 us
    all_to_all x1, waiting for transfers between devices, shards(): lax.all_to_all(pieces, both, 0, 0, tiled=True, axis_index_groups=SAME_CORE)  27.3 us
    all_to_all x1, blocking collectives, shards(): lax.all_to_all(pieces, both, 0, 0, tiled=True, axis_index_groups=SAME_CORE)  22 us
    pallas_call x1, Pallas kernels, gradient_pieces(): pl.pallas_call(gradient_kernel, out_shape=jax.ShapeDtypeStruct((64, 8, 16...  11.1 us
    unnamed x14, local copies, waits for them, and re-layouts  9.92 us
    pallas_call x1, Pallas kernels, newton(): pl.pallas_call(newton_kernel, out_shape=jax.ShapeDtypeStruct((BLOCK, BLOC...  9.7 us
    ppermute x1, waiting for transfers between devices, shards(): other_features = lax.ppermute(features, 'grp', CORE)  5.73 us
    pallas_call x1, Pallas kernels, route(): pl.pallas_call(route_kernel, out_shape=jax.ShapeDtypeStruct((64, 4, 16, 1...  5.69 us
  transfers between devices with their start and end apart: 6, of which 5 were waited for; matrix products, arithmetic and copies ran while one was open for 1% of the time, Pallas kernels for 4%

profile of v1, /device:TPU:1, one launch (start us, length us, event | category | flops | bytes accessed | tf_op | source)
XLA Modules:
  0.0 177.0 jit_solution(15147035088255195699)
XLA Ops:
  0.0 0.0 copy-start
  0.0 0.7 convert_bitcast_fusion
  0.7 0.3 copy-done
  1.0 0.4 broadcast_in_dim.2
  1.5 0.0 copy-start.3
  1.5 53.4 %all_to_all.15.own = bf16[32,400,128]{2,1,0:T(8,128)(2,1)} all-to-all(bf16[32,400,128]{2,1,0:T(8,128)(2,1)S(1)} %broadcast_in_dim.2), channel_id=1, replica_groups=mesh['grp'=4,'dev'=32] {'dev'}, dimensions={0} | all-to-all | bytes 6553600 | tf_op jit(solution)/shard_map/all_to_all | solution.py:365
  54.9 2.2 %collective-permute-start = (bf16[32,400,128]{2,1,0:T(8,128)(2,1)}, bf16[32,400,128]{2,1,0:T(8,128)(2,1)}, u32[]{:S(2)}, u32[]{:S(2)}) collective-permute-start(bf16[32,400,128]{2,1,0:T(8,128)(2,1)} %all_to_all.15.own), channel_id=1, source_target_pairs={{0,32},{32,0},{64,96},{96,64},{1,33},{33,1},{65,97},{97,65},{2,34}... | collective-permute-start | bytes 9830408 | tf_op jit(solution)/shard_map/ppermute | solution.py:367
  57.1 0.1 stack.23.where
  57.1 5.7 %collective-permute-done.other = bf16[32,400,128]{2,1,0:T(8,128)(2,1)} collective-permute-done((bf16[32,400,128]{2,1,0:T(8,128)(2,1)}, bf16[32,400,128]{2,1,0:T(8,128)(2,1)}, u32[]{:S(2)}, u32[]{:S(2)}) %collective-permute-start) | collective-permute-done | bytes 3276832 | tf_op jit(solution)/shard_map/ppermute | solution.py:367
  62.9 0.0 copy-done.3
  62.9 0.0 copy-start.4
  62.9 2.2 %copy-done.4 = bf16[4096,512]{1,0:T(8,128)(2,1)S(1)} copy-done((bf16[4096,512]{1,0:T(8,128)(2,1)S(1)}, bf16[4096,512]{1,0:T(8,128)(2,1)}, u32[]{:S(2)}) %copy-start.4) | copy-done | bytes 4194328
  65.1 11.1 %gradient.1 = bf16[64,8,16,128]{3,2,1,0:T(8,128)(2,1)} custom-call(s32[5]{0:T(128)S(1)} %stack.23.where, bf16[32,400,128]{2,1,0:T(8,128)(2,1)} %all_to_all.15.own, bf16[32,400,128]{2,1,0:T(8,128)(2,1)} %collective-permute-done.other, bf16[4096,512]{1,0:T(8,128)(2,1)S(1)} %copy-done.4, bf16[1536,512]{1,0:T(8,128)(2,1)S(1)} %copy-done.3, ...), custom_call_target="tpu_custom_call" | custom-call | tf_op jit(solution)/shard_map/gradient/pallas_call | solution.py:131
  76.2 0.0 copy-start.6
  76.2 4.8 %all-to-all-start.1 = ((bf16[64,8,16,128]{3,2,1,0:T(8,128)(2,1)}), bf16[64,8,16,128]{3,2,1,0:T(8,128)(2,1)S(1)}, u32[]{:S(2)}, u32[]{:S(2)}) async-start(bf16[64,8,16,128]{3,2,1,0:T(8,128)(2,1)} %gradient.1), calls=%async_computation.1 | async-start | bytes 4194304 | tf_op jit(solution)/shard_map/all_to_all | solution.py:370
  81.0 0.9 fusion.2
  81.9 0.1 reshape.9.ids
  82.0 27.3 %all-to-all-done.1.pieces = bf16[64,8,16,128]{3,2,1,0:T(8,128)(2,1)S(1)} async-done(((bf16[64,8,16,128]{3,2,1,0:T(8,128)(2,1)}), bf16[64,8,16,128]{3,2,1,0:T(8,128)(2,1)S(1)}, u32[]{:S(2)}, u32[]{:S(2)}) %all-to-all-start.1) | async-done | bytes 2097184 | tf_op jit(solution)/shard_map/all_to_all | solution.py:370
  109.3 0.0 copy-done.6
  109.3 5.7 %route.1 = bf16[64,4,16,128]{3,2,1,0:T(8,128)(2,1)S(1)} custom-call(s32[256]{0:T(256)S(1)} %reshape.9.ids, s32[32]{0:T(128)S(1)} %copy-done.6, bf16[64,8,16,128]{3,2,1,0:T(8,128)(2,1)S(1)} %all-to-all-done.1.pieces), custom_call_target="tpu_custom_call" | custom-call | tf_op jit(solution)/shard_map/route/pallas_call | solution.py:175
  115.0 22.0 %all_to_all.16.mine = bf16[64,4,16,128]{3,2,1,0:T(8,128)(2,1)S(1)} all-to-all(bf16[64,4,16,128]{3,2,1,0:T(8,128)(2,1)S(1)} %route.1), channel_id=1, replica_groups={{0,1,2,3,4,5,6,7,8,9,10,11,12,13,14,15,16,17,18,19,20,21,22,23,24,25,26..., dimensions={0} | all-to-all | bytes 2097152 | tf_op jit(solution)/shard_map/all_to_all | solution.py:372
  137.0 3.2 %collective-permute-start.1 = (bf16[64,4,16,128]{3,2,1,0:T(8,128)(2,1)S(1)}, bf16[64,4,16,128]{3,2,1,0:T(8,128)(2,1)S(1)}, u32[]{:S(2)}, u32[]{:S(2)}) collective-permute-start(bf16[64,4,16,128]{3,2,1,0:T(8,128)(2,1)S(1)} %all_to_all.16.mine), channel_id=1, source_target_pairs={{0,32},{32,0},{64,96},{96,64},{1,33},{33,1},{65,97},{97,65},{2,34}... | collective-permute-start | bytes 3145736 | tf_op jit(solution)/shard_map/ppermute | solution.py:373
  140.2 1.6 plan.1.slot_at
  141.8 0.7 collective-permute-done.1.theirs
  142.5 0.0 copy-start.5
  142.5 0.7 copy-done.5
  143.1 9.7 %newton.1.root = bf16[512,512]{1,0:T(8,128)(2,1)S(1)} custom-call(s32[5]{0:T(128)S(1)} %stack.23.where, s32[16]{0:T(128)S(1)} %copy-done.5, bf16[64,4,16,128]{3,2,1,0:T(8,128)(2,1)S(1)} %all_to_all.16.mine, bf16[64,4,16,128]{3,2,1,0:T(8,128)(2,1)S(1)} %collective-permute-done.1.theirs, bf16[8,2,512,512]{3,2,1,0:T(8,128)(2,1)} %statistic.1), custom_call_target="tpu_custom_call" | custom-call | tf_op jit(solution)/shard_map/newton/pallas_call | solution.py:274
  152.8 1.1 collective-permute-start.2
  154.0 0.0 copy-start.1
  154.0 3.4 %copy-done.1 = bf16[8,2,512,512]{3,2,1,0:T(8,128)(2,1)S(1)} copy-done((bf16[8,2,512,512]{3,2,1,0:T(8,128)(2,1)S(1)}, bf16[8,2,512,512]{3,2,1,0:T(8,128)(2,1)}, u32[]{:S(2)}) %copy-start.1) | copy-done | bytes 8388632
  157.4 4.4 %stored.1 = (bf16[3,128,512]{2,1,0:T(8,128)(2,1)S(1)}, bf16[3,128,512]{2,1,0:T(8,128)(2,1)S(1)}) custom-call(s32[5]{0:T(128)S(1)} %stack.23.where, s32[16]{0:T(128)S(1)} %copy-done.5, bf16[64,4,16,128]{3,2,1,0:T(8,128)(2,1)S(1)} %all_to_all.16.mine, bf16[64,4,16,128]{3,2,1,0:T(8,128)(2,1)S(1)} %collective-permute-done.1.theirs, ...), custom_call_target="tpu_custom_call" | custom-call | tf_op jit(solution)/shard_map/stored/pallas_call | solution.py:215
  161.8 0.6 collective-permute-start.4
  162.4 0.0 collective-permute-done.2.other_root
  162.4 0.0 copy-start.2
  162.4 3.4 %copy-done.2 = bf16[8,2,512,512]{3,2,1,0:T(8,128)(2,1)S(1)} copy-done((bf16[8,2,512,512]{3,2,1,0:T(8,128)(2,1)S(1)}, bf16[8,2,512,512]{3,2,1,0:T(8,128)(2,1)}, u32[]{:S(2)}) %copy-start.2) | copy-done | bytes 8388632
  165.8 1.9 %fresh.1 = (bf16[1,128,512]{2,1,0:T(8,128)(2,1)S(1)}, bf16[1,128,512]{2,1,0:T(8,128)(2,1)S(1)}) custom-call(s32[5]{0:T(128)S(1)} %stack.23.where, s32[16]{0:T(128)S(1)} %copy-done.5, bf16[64,4,16,128]{3,2,1,0:T(8,128)(2,1)S(1)} %all_to_all.16.mine, bf16[64,4,16,128]{3,2,1,0:T(8,128)(2,1)S(1)} %collective-permute-done.1.theirs, ...), custom_call_target="tpu_custom_call" | custom-call | tf_op jit(solution)/shard_map/fresh/pallas_call | solution.py:306
  167.7 1.0 collective-permute-start.3
  168.7 3.9 %collective-permute-done.4.theirs = bf16[3,128,512]{2,1,0:T(8,128)(2,1)S(1)} collective-permute-done((bf16[3,128,512]{2,1,0:T(8,128)(2,1)S(1)}, bf16[3,128,512]{2,1,0:T(8,128)(2,1)S(1)}, u32[]{:S(2)}, u32[]{:S(2)}) %collective-permute-start.4) | collective-permute-done | bytes 393248 | tf_op jit(solution)/shard_map/ppermute | solution.py:376
  172.6 2.8 %collective-permute-done.3.fresh_theirs = bf16[1,128,512]{2,1,0:T(8,128)(2,1)S(1)} collective-permute-done((bf16[1,128,512]{2,1,0:T(8,128)(2,1)S(1)}, bf16[1,128,512]{2,1,0:T(8,128)(2,1)S(1)}, u32[]{:S(2)}, u32[]{:S(2)}) %collective-permute-start.3) | collective-permute-done | bytes 131104 | tf_op jit(solution)/shard_map/ppermute | solution.py:380
  175.4 1.6 assemble.1
  (2 shorter events, 0.0 us)
Async XLA Ops:
  0.0 1.0 copy-start
  1.5 61.4 %copy-start.3 = (bf16[1536,512]{1,0:T(8,128)(2,1)S(1)}, bf16[1536,512]{1,0:T(8,128)(2,1)}, u32[]{:S(2)}) copy-start(bf16[1536,512]{1,0:T(8,128)(2,1)} %up_other.1) | copy-start | bytes 4718596
  54.9 8.0 %collective-permute-start = (bf16[32,400,128]{2,1,0:T(8,128)(2,1)}, bf16[32,400,128]{2,1,0:T(8,128)(2,1)}, u32[]{:S(2)}, u32[]{:S(2)}) collective-permute-start(bf16[32,400,128]{2,1,0:T(8,128)(2,1)} %all_to_all.15.own), channel_id=1, source_target_pairs={{0,32},{32,0},{64,96},{96,64},{1,33},{33,1},{65,97},{97,65},{2,34}... | collective-permute-start | bytes 9830408 | tf_op jit(solution)/shard_map/ppermute | solution.py:367
  62.9 2.2 %copy-start.4 = (bf16[4096,512]{1,0:T(8,128)(2,1)S(1)}, bf16[4096,512]{1,0:T(8,128)(2,1)}, u32[]{:S(2)}) copy-start(bf16[4096,512]{1,0:T(8,128)(2,1)} %weight.1) | copy-start | bytes 12582916
  76.2 33.1 %copy-start.6 = (s32[32]{0:T(128)S(1)}, s32[32]{0:T(128)}, u32[]{:S(2)}) copy-start(s32[32]{0:T(128)} %refreshed.3) | copy-start | bytes 388
  76.2 33.1 %all-to-all-start.1 = ((bf16[64,8,16,128]{3,2,1,0:T(8,128)(2,1)}), bf16[64,8,16,128]{3,2,1,0:T(8,128)(2,1)S(1)}, u32[]{:S(2)}, u32[]{:S(2)}) async-start(bf16[64,8,16,128]{3,2,1,0:T(8,128)(2,1)} %gradient.1), calls=%async_computation.1 | async-start | bytes 4194304 | tf_op jit(solution)/shard_map/all_to_all | solution.py:370
  137.0 5.5 %collective-permute-start.1 = (bf16[64,4,16,128]{3,2,1,0:T(8,128)(2,1)S(1)}, bf16[64,4,16,128]{3,2,1,0:T(8,128)(2,1)S(1)}, u32[]{:S(2)}, u32[]{:S(2)}) collective-permute-start(bf16[64,4,16,128]{3,2,1,0:T(8,128)(2,1)S(1)} %all_to_all.16.mine), channel_id=1, source_target_pairs={{0,32},{32,0},{64,96},{96,64},{1,33},{33,1},{65,97},{97,65},{2,34}... | collective-permute-start | bytes 3145736 | tf_op jit(solution)/shard_map/ppermute | solution.py:373
  142.5 0.7 copy-start.5
  152.8 9.6 %collective-permute-start.2 = (bf16[512,512]{1,0:T(8,128)(2,1)S(1)}, bf16[512,512]{1,0:T(8,128)(2,1)S(1)}, u32[]{:S(2)}, u32[]{:S(2)}) collective-permute-start(bf16[512,512]{1,0:T(8,128)(2,1)S(1)} %newton.1.root), channel_id=1, source_target_pairs={{0,32},{32,0},{64,96},{96,64},{1,33},{33,1},{65,97},{97,65},{2,34}... | collective-permute-start | bytes 1572872 | tf_op jit(solution)/shard_map/ppermute | solution.py:378
  154.0 3.4 %copy-start.1 = (bf16[8,2,512,512]{3,2,1,0:T(8,128)(2,1)S(1)}, bf16[8,2,512,512]{3,2,1,0:T(8,128)(2,1)}, u32[]{:S(2)}) copy-start(bf16[8,2,512,512]{3,2,1,0:T(8,128)(2,1)} %roots.3) | copy-start | bytes 25165828
  161.8 10.8 %collective-permute-start.4 = (bf16[3,128,512]{2,1,0:T(8,128)(2,1)S(1)}, bf16[3,128,512]{2,1,0:T(8,128)(2,1)S(1)}, u32[]{:S(2)}, u32[]{:S(2)}) collective-permute-start(bf16[3,128,512]{2,1,0:T(8,128)(2,1)S(1)} %get-tuple-element.12), channel_id=1, source_target_pairs={{0,64},{64,0},{32,96},{96,32},{1,65},{65,1},{33,97},{97,33},{2,66}... | collective-permute-start | bytes 1179656 | tf_op jit(solution)/shard_map/ppermute | solution.py:376
  162.4 3.4 %copy-start.2 = (bf16[8,2,512,512]{3,2,1,0:T(8,128)(2,1)S(1)}, bf16[8,2,512,512]{3,2,1,0:T(8,128)(2,1)}, u32[]{:S(2)}) copy-start(bf16[8,2,512,512]{3,2,1,0:T(8,128)(2,1)} %roots.3) | copy-start | bytes 25165828
  167.7 7.7 %collective-permute-start.3 = (bf16[1,128,512]{2,1,0:T(8,128)(2,1)S(1)}, bf16[1,128,512]{2,1,0:T(8,128)(2,1)S(1)}, u32[]{:S(2)}, u32[]{:S(2)}) collective-permute-start(bf16[1,128,512]{2,1,0:T(8,128)(2,1)S(1)} %get-tuple-element.10), channel_id=1, source_target_pairs={{0,64},{64,0},{32,96},{96,32},{1,65},{65,1},{33,97},{97,33},{2,66}... | collective-permute-start | bytes 393224 | tf_op jit(solution)/shard_map/ppermute | solution.py:380
